TPU v7x, 32 devices: a whole 2x2x4 slice. The times are simulated.
32 devices in a mesh: ka: 8 (over z, y), ga: 4 (over x, core).
Axes of the slice: x: 2, y: 2, z: 4, core: 2. Of those that a mesh axis runs over, the one named last changes fastest.
Arguments:
- cond: bfloat16 [8, 8, 4096], P('ka', None, 'ga'), may hold values from -6 to 6
- vale: bfloat16 [8, 8, 4096], P('ka', None, 'ga'), may hold values from -6 to 6
- screen: bfloat16 [8, 4096, 4096], P('ka', 'ga'), may hold values from -0.0014648438 to 0.0014648438
- qtable: int32 [8, 8], replicated, may hold values from 0 to 7, as said below
- gmap: int32 [8, 4096], P('ka', 'ga'), may hold values from 0 to 4095, as said below
Outputs:
- kernel: float32 [8, 3, 4096], P('ka', None, 'ga')
Inputs may be any that keep to these rules, and one draw needn't show every extreme that they name: qtable[k,k2] depends only on (k - k2) mod 8, and each row names every k-difference once. `gmap`: each aligned block of 1024 entries of a row is an ordering of that block's own grid indices.
All inputs are finite; a program needn't handle non-finite values.
Results may differ from a plain program's by a relative error of at most 0.0041.
Values may be sent and summed in bfloat16 or wider, within the bound.
A program may use at most 128 MiB of HBM per device.

v0:
```python
import functools

import jax
import jax.numpy as jnp
from jax import lax
from jax.experimental import pallas as pl
from jax.experimental.pallas import tpu as pltpu
from jax.sharding import PartitionSpec as P

NSHIFT = 2
MESH = pl.DeviceIdType.MESH
F32 = jnp.float32
BF16 = jnp.bfloat16


def flipped(index, bit):
    width = 1 << bit
    return index + width * (1 - 2 * ((index // width) % 2))


def moved(index, offset, bits):
    for bit in range(bits):
        if (offset >> bit) & 1:
            index = flipped(index, bit)
    return index


def densities(own, far):
    product = own.astype(F32)[:, None, :] * far.astype(F32)[None, :, :]
    return product.reshape(-1, own.shape[-1]).astype(BF16)


def kernel(
    n_k, n_g, cond_in, vale_in, screen, qtable_in, gmap_in, out,
    cond, vale, qtable, gmap, s_held, c_all, pc, tiles, sent, got,
    in_sem, s_sem, c_send, c_recv, v_send, v_recv, g_send, g_recv,
    t_send, t_recv, *blocks,
):
    v_from, w_from = blocks[:n_g], blocks[n_g:]
    bits = n_g.bit_length() - 1
    width = cond.shape[2]
    n_c = cond.shape[1]
    rows = n_c * n_c
    total = n_k * n_g
    me_k, me_g = lax.axis_index("ka"), lax.axis_index("ga")
    me = me_k * n_g + me_g

    arrivals = [
        pltpu.make_async_copy(source, target, in_sem.at[number])
        for number, (source, target) in enumerate(
            [(gmap_in, gmap), (cond_in, cond), (vale_in, vale), (qtable_in, qtable)]
        )
    ]
    for arrival in arrivals:
        arrival.start()

    barrier = pltpu.get_barrier_semaphore()

    def greet(step, carry):
        peer = (me + step) % total
        pl.semaphore_signal(
            barrier, inc=1, device_id=(peer // n_g, peer % n_g), device_id_type=MESH
        )
        return carry

    lax.fori_loop(1, total, greet, 0)

    loads = []
    for offset in range(n_g):
        block = moved(me_g, offset, bits)
        load = pltpu.make_async_copy(
            screen.at[0, :, pl.ds(pl.multiple_of(block * width, width), width)],
            s_held.at[block],
            s_sem.at[offset],
        )
        load.start()
        loads.append(load)

    for arrival in arrivals:
        arrival.wait()

    local_map = gmap[...] - me_g * width
    both = jnp.concatenate([cond[0], vale[0]], axis=0)
    lanes = min(128, width)
    points = lax.broadcasted_iota(jnp.int32, (lanes, width), 0)
    pick = jnp.where(points == local_map % lanes, 1.0, 0.0).astype(BF16)
    stacked = jnp.concatenate(
        [both[:, first : first + lanes] for first in range(0, width, lanes)], axis=0
    )
    spread = jnp.dot(stacked, pick, preferred_element_type=F32)
    mapped = jnp.zeros((2 * n_c, width), F32)
    for number in range(width // lanes):
        piece = spread[number * 2 * n_c : (number + 1) * 2 * n_c]
        mapped = jnp.where(local_map // lanes == number, piece, mapped)
    mapped = mapped.astype(BF16)
    c_all[me_k] = jnp.concatenate([cond[0], mapped[:n_c]], axis=0)
    v_from[0][me_k] = jnp.concatenate([vale[0], mapped[n_c:]], axis=0)

    pl.semaphore_wait(barrier, total - 1)

    depth = n_k // 2
    me_z, me_y = me_k // 2, me_k % 2
    other = me_z * 2 + 1 - me_y

    def along(step):
        return ((me_z + step) % depth) * 2 + me_y

    def beside(step):
        return ((me_z + step) % depth) * 2 + 1 - me_y

    def c_copy(chunk, slot, target):
        return pltpu.make_async_remote_copy(
            src_ref=c_all.at[chunk], dst_ref=c_all.at[chunk],
            send_sem=c_send.at[slot], recv_sem=c_recv.at[chunk],
            device_id=(target, me_g), device_id_type=MESH,
        )

    def v_copy(chunk, slot, target):
        return pltpu.make_async_remote_copy(
            src_ref=v_from[0].at[chunk], dst_ref=v_from[0].at[chunk],
            send_sem=v_send.at[slot], recv_sem=v_recv.at[chunk],
            device_id=(target, me_g), device_id_type=MESH,
        )

    def across(chunk):
        for bit in reversed(range(bits)):
            pltpu.make_async_remote_copy(
                src_ref=v_from[0].at[chunk], dst_ref=v_from[1 << bit].at[chunk],
                send_sem=g_send.at[1 << bit], recv_sem=g_recv.at[1 << bit],
                device_id=(me_k, flipped(me_g, bit)), device_id_type=MESH,
            ).start()

    def whole_block(offset, bit):
        return pltpu.make_async_remote_copy(
            src_ref=v_from[offset], dst_ref=v_from[offset | (1 << bit)],
            send_sem=g_send.at[offset | (1 << bit)], recv_sem=g_recv.at[offset | (1 << bit)],
            device_id=(me_k, flipped(me_g, bit)), device_id_type=MESH,
        )

    for step in range(1, depth):
        c_copy(me_k, step - 1, along(step)).start()
    c_copy(me_k, depth - 1, other).start()
    across(me_k)
    for step in range(1, depth):
        c_copy(along(step), 0, other).wait_recv()
        c_copy(along(step), depth - 1 + step, other).start()
    for step in range(1, depth):
        v_copy(me_k, step - 1, along(step)).start()
    v_copy(me_k, depth - 1, other).start()
    for step in range(depth):
        c_copy(beside(step), 0, other).wait_recv()

    shift = jnp.int32(0)
    for row in range(n_k):
        shift = jnp.where(qtable[row, 0] == me_k, row, shift)

    def build(k, carry):
        partner = lax.rem(k - shift + n_k, n_k)
        dens = densities(c_all[k][:n_c], c_all[partner][n_c:])
        pc[pl.ds(pl.multiple_of(k * rows, rows), rows), :] = dens
        return carry

    lax.fori_loop(0, n_k, build, 0)
    tiles[...] = jnp.zeros_like(tiles)

    sub = min(512, width)
    unit = 8
    group = 4
    cuts = width // sub

    def work(weigh, close):
        if weigh is not None:
            block = moved(me_g, weigh, bits)
            loads[weigh].wait()

        def step(number, carry):
            which, column = number // cuts, number % cuts
            columns = pl.ds(pl.multiple_of(column * sub, sub), sub)
            all_rows = pl.ds(pl.multiple_of(which * (unit * rows), unit * rows), unit * rows)
            if weigh is not None:
                w_from[weigh][all_rows, columns] = jnp.dot(
                    pc[all_rows, :], s_held[block, :, columns], preferred_element_type=F32
                ).astype(BF16)
            if close is not None:
                for part in range(unit // group):
                    dens = []
                    for k in range(group):
                        k = which * unit + part * group + k
                        partner = lax.rem(k - shift + n_k, n_k)
                        own = v_from[close][k, :, columns][:n_c]
                        far = v_from[close][partner, :, columns][n_c:]
                        dens.append(densities(own, far))
                    first = pl.multiple_of((which * unit + part * group) * rows, group * rows)
                    tiles[which * (unit // group) + part] += lax.dot_general(
                        w_from[close][pl.ds(first, group * rows), columns],
                        jnp.concatenate(dens, axis=0),
                        (((1,), (1,)), ((), ())),
                        preferred_element_type=F32,
                    )
            return carry

        lax.fori_loop(0, (n_k // unit) * cuts, step, 0)

    passed = {0}

    def pass_on(offset):
        if offset in passed:
            return
        passed.add(offset)
        low = (offset & -offset).bit_length() - 1
        whole_block(offset & (offset - 1), low).wait_recv()
        for bit in reversed(range(low)):
            whole_block(offset, bit).start()

    order = sorted(range(n_g), key=lambda offset: (bin(offset).count("1"), offset))
    work(order[0], None)
    for step in range(1, depth):
        v_copy(along(step), 0, other).wait_recv()
        v_copy(along(step), depth - 1 + step, other).start()
        across(along(step))
    work(order[1], None)
    for step in range(depth):
        v_copy(beside(step), 0, other).wait_recv()
        across(beside(step))
    for number in range(2, n_g):
        if number > 2:
            pass_on(order[number - 2])
            pass_on(order[number - 1])
        work(order[number], order[number - 2])
    for offset in order[n_g - 2 :]:
        pass_on(offset)
        work(None, offset)

    share = rows // n_g
    half = share // 2

    def lay_out(which, carry):
        for k in range(group):
            for to in range(n_g):
                first = k * rows + to * share
                lanes = slice(k * rows, (k + 1) * rows)
                sent[(which * group + k) * n_g + to] = jnp.concatenate(
                    [
                        tiles[which, first : first + half, lanes],
                        tiles[which, first + half : first + share, lanes],
                    ],
                    axis=1,
                )
        return carry

    lax.fori_loop(0, n_k // group, lay_out, 0)

    def hand_out(step, carry):
        peer = (me + step) % total
        pltpu.make_async_remote_copy(
            src_ref=sent.at[peer], dst_ref=got.at[me],
            send_sem=t_send, recv_sem=t_recv,
            device_id=(peer // n_g, peer % n_g), device_id_type=MESH,
        ).start()
        return carry

    lax.fori_loop(1, total, hand_out, 0)
    got[me] = sent[me]

    for slot in range(n_k - 1):
        c_copy(me_k, slot, other).wait_send()
        v_copy(me_k, slot, other).wait_send()
    for offset in range(1, n_g):
        low = (offset & -offset).bit_length() - 1
        whole_block(offset & (offset - 1), low).wait_send()

    handed = pltpu.make_async_remote_copy(
        src_ref=sent.at[pl.ds(0, total - 1)], dst_ref=got.at[pl.ds(0, total - 1)],
        send_sem=t_send, recv_sem=t_recv,
        device_id=(other, me_g), device_id_type=MESH,
    )
    handed.wait_recv()
    for number in range(NSHIFT + 1):
        holder = qtable[number, 0]
        value = got[holder * n_g]
        for source in range(1, n_g):
            value += got[holder * n_g + source]
        for row in range(share):
            side = row // half
            first = row - side * half
            out[0, number : number + 1, row * rows : (row + 1) * rows] = value[
                first : first + 1, side * rows : (side + 1) * rows
            ]
    handed.wait_send()


def per_device(cond, vale, screen, qtable, gmap):
    n_k, n_g = lax.axis_size("ka"), lax.axis_size("ga")
    n_c, width = cond.shape[1], cond.shape[2]
    rows = n_c * n_c
    share = rows // n_g
    total = n_k * n_g
    anywhere = pl.BlockSpec(memory_space=pltpu.HBM)
    dma = pltpu.SemaphoreType.DMA
    return pl.pallas_call(
        functools.partial(kernel, n_k, n_g),
        out_shape=jax.ShapeDtypeStruct((1, NSHIFT + 1, share * rows), F32),
        in_specs=[anywhere] * 5,
        out_specs=pl.BlockSpec(memory_space=pltpu.VMEM),
        scratch_shapes=[
            pltpu.VMEM(cond.shape, BF16),
            pltpu.VMEM(vale.shape, BF16),
            pltpu.SMEM(qtable.shape, jnp.int32),
            pltpu.VMEM(gmap.shape, jnp.int32),
            pltpu.VMEM((n_g, width, width), BF16),
            pltpu.VMEM((n_k, 2 * n_c, width), BF16),
            pltpu.VMEM((n_k * rows, width), BF16),
            pltpu.VMEM((n_k // 4, 4 * rows, 4 * rows), F32),
            pltpu.VMEM((total, share // 2, 2 * rows), F32),
            pltpu.VMEM((total, share // 2, 2 * rows), F32),
            dma((4,)), dma((n_g,)), dma((n_k,)), dma((n_k,)), dma((n_k,)), dma((n_k,)),
            dma((n_g,)), dma((n_g,)), dma(()), dma(()),
        ]
        + [pltpu.VMEM((n_k, 2 * n_c, width), BF16)] * n_g
        + [pltpu.VMEM((n_k * rows, width), BF16)] * n_g,
        compiler_params=pltpu.CompilerParams(
            collective_id=0, has_side_effects=True, vmem_limit_bytes=63 * 1024 * 1024
        ),
        cost_estimate=pl.CostEstimate(
            flops=2 * n_k * rows * width * screen.shape[2],
            bytes_accessed=2 * width * screen.shape[2],
            transcendentals=0,
        ),
    )(cond, vale, screen, qtable, gmap)


def solution(mesh):
    in_specs = (P("ka", None, "ga"), P("ka", None, "ga"), P("ka", "ga", None), P(), P("ka", "ga"))
    out_specs = P("ka", None, "ga")
    return jax.shard_map(
        per_device, mesh=mesh, in_specs=in_specs, out_specs=out_specs, check_vma=False
    )
```

profile of v0, /device:TPU:0, one launch (start us, length us, event | category | flops | bytes accessed | tf_op | source)
XLA Modules:
  0.0 33.7 jit_solution(650424000177329183)
XLA Ops:
  0.0 32.4 %shard_map.55 = f32[1,3,1024]{2,1,0:T(4,128)} custom-call(bf16[1,8,1024]{2,1,0:T(8,128)(2,1)} %cond_in.1, bf16[1,8,1024]{2,1,0:T(8,128)(2,1)} %vale_in.1, bf16[1,1024,4096]{2,1,0:T(8,128)(2,1)} %screen.1, s32[8,8]{1,0:T(8,128)} %qtable_in.1, s32[1,1024]{1,0:T(1,128)} %gmap_in.1), custom_call_target="tpu_custom_call" | custom-call | flops 4294967296 | bytes 8388608 | tf_op jit(solution)/shard_map/pallas_call | solution.py:300
  32.4 1.3 %copy.6 = f32[1,3,1024]{2,0,1:T(1,128)} copy(f32[1,3,1024]{2,1,0:T(4,128)} %shard_map.55) | data formatting | bytes 24576 | tf_op jit(solution)/shard_map/pallas_call | solution.py:300
where the time goes:
time: 34 us; the launch traced here: 33.7 us
  Pallas kernels  32.4 us (95%)
  local copies, waits for them, and re-layouts  1.33 us (4%)
    pallas_call x1, Pallas kernels, per_device(): pl.pallas_call(functools.partial(kernel, n_k, n_g), out_shape=jax.ShapeDt...  32.4 us
    pallas_call x1, local copies, waits for them, and re-layouts, per_device(): pl.pallas_call(functools.partial(kernel, n_k, n_g), out_shape=jax.ShapeDt...  1.33 us

commit v1 on v0

--- a/solution.py
+++ b/solution.py
@@ -54,16 +54,21 @@
     for arrival in arrivals:
         arrival.start()
 
+    depth = n_k // 2
+    me_z, me_y = me_k // 2, me_k % 2
+    other = me_z * 2 + 1 - me_y
+
+    def along(step):
+        return ((me_z + step) % depth) * 2 + me_y
+
+    def beside(step):
+        return ((me_z + step) % depth) * 2 + 1 - me_y
+
     barrier = pltpu.get_barrier_semaphore()
-
-    def greet(step, carry):
-        peer = (me + step) % total
-        pl.semaphore_signal(
-            barrier, inc=1, device_id=(peer // n_g, peer % n_g), device_id_type=MESH
-        )
-        return carry
-
-    lax.fori_loop(1, total, greet, 0)
+    peers = [(along(step), me_g) for step in range(1, depth)] + [(other, me_g)]
+    peers += [(me_k, flipped(me_g, bit)) for bit in range(bits)]
+    for peer in peers:
+        pl.semaphore_signal(barrier, inc=1, device_id=peer, device_id_type=MESH)
 
     loads = []
     for offset in range(n_g):
@@ -96,17 +101,7 @@
     c_all[me_k] = jnp.concatenate([cond[0], mapped[:n_c]], axis=0)
     v_from[0][me_k] = jnp.concatenate([vale[0], mapped[n_c:]], axis=0)
 
-    pl.semaphore_wait(barrier, total - 1)
-
-    depth = n_k // 2
-    me_z, me_y = me_k // 2, me_k % 2
-    other = me_z * 2 + 1 - me_y
-
-    def along(step):
-        return ((me_z + step) % depth) * 2 + me_y
-
-    def beside(step):
-        return ((me_z + step) % depth) * 2 + 1 - me_y
+    pl.semaphore_wait(barrier, len(peers))
 
     def c_copy(chunk, slot, target):
         return pltpu.make_async_remote_copy(
@@ -229,37 +224,57 @@
         work(order[number], order[number - 2])
     for offset in order[n_g - 2 :]:
         pass_on(offset)
-        work(None, offset)
 
     share = rows // n_g
     half = share // 2
-
-    def lay_out(which, carry):
+    n_groups = n_k // group
+
+    def finish(number, carry):
+        which = (me_k // group + number) % n_groups
+        tile = tiles[which]
+        first = pl.multiple_of(which * (group * rows), group * rows)
+        for close in order[n_g - 2 :]:
+            for cut in range(cuts):
+                columns = slice(cut * sub, (cut + 1) * sub)
+                dens = []
+                for k in range(group):
+                    k = which * group + k
+                    partner = lax.rem(k - shift + n_k, n_k)
+                    own = v_from[close][k, :, columns][:n_c]
+                    far = v_from[close][partner, :, columns][n_c:]
+                    dens.append(densities(own, far))
+                tile += lax.dot_general(
+                    w_from[close][pl.ds(first, group * rows), columns],
+                    jnp.concatenate(dens, axis=0),
+                    (((1,), (1,)), ((), ())),
+                    preferred_element_type=F32,
+                )
         for k in range(group):
             for to in range(n_g):
-                first = k * rows + to * share
+                top = k * rows + to * share
                 lanes = slice(k * rows, (k + 1) * rows)
                 sent[(which * group + k) * n_g + to] = jnp.concatenate(
-                    [
-                        tiles[which, first : first + half, lanes],
-                        tiles[which, first + half : first + share, lanes],
-                    ],
+                    [tile[top : top + half, lanes], tile[top + half : top + share, lanes]],
                     axis=1,
                 )
+
+        def hand_out(step, carry):
+            peer = which * (group * n_g) + step
+
+            @pl.when(peer != me)
+            def _():
+                pltpu.make_async_remote_copy(
+                    src_ref=sent.at[peer], dst_ref=got.at[me],
+                    send_sem=t_send, recv_sem=t_recv,
+                    device_id=(peer // n_g, peer % n_g), device_id_type=MESH,
+                ).start()
+
+            return carry
+
+        lax.fori_loop(0, group * n_g, hand_out, 0)
         return carry
 
-    lax.fori_loop(0, n_k // group, lay_out, 0)
-
-    def hand_out(step, carry):
-        peer = (me + step) % total
-        pltpu.make_async_remote_copy(
-            src_ref=sent.at[peer], dst_ref=got.at[me],
-            send_sem=t_send, recv_sem=t_recv,
-            device_id=(peer // n_g, peer % n_g), device_id_type=MESH,
-        ).start()
-        return carry
-
-    lax.fori_loop(1, total, hand_out, 0)
+    lax.fori_loop(1, n_groups + 1, finish, 0)
     got[me] = sent[me]
 
     for slot in range(n_k - 1):

time: 34 us -> 31.4 us (0.924)
  Pallas kernels: 32.4 us -> 29.8 us
    pallas_call x1, Pallas kernels: 32.4 us -> 29.8 us  [per_device(): pl.pallas_call(functools.partial(kernel, n_k, n_g), out_shape=jax.ShapeDt...]
where the time goes in v1:
time: 31.4 us; the launch traced here: 31.1 us
  Pallas kernels  29.8 us (95%)
  local copies, waits for them, and re-layouts  1.33 us (4%)
    pallas_call x1, Pallas kernels, per_device(): pl.pallas_call(functools.partial(kernel, n_k, n_g), out_shape=jax.ShapeDt...  29.8 us
    pallas_call x1, local copies, waits for them, and re-layouts, per_device(): pl.pallas_call(functools.partial(kernel, n_k, n_g), out_shape=jax.ShapeDt...  1.33 us

profile of v1, /device:TPU:0, one launch (start us, length us, event | category | flops | bytes accessed | tf_op | source)
XLA Modules:
  0.0 31.1 jit_solution(12851320521350882008)
XLA Ops:
  0.0 29.8 %shard_map.55 = f32[1,3,1024]{2,1,0:T(4,128)} custom-call(bf16[1,8,1024]{2,1,0:T(8,128)(2,1)} %cond_in.1, bf16[1,8,1024]{2,1,0:T(8,128)(2,1)} %vale_in.1, bf16[1,1024,4096]{2,1,0:T(8,128)(2,1)} %screen.1, s32[8,8]{1,0:T(8,128)} %qtable_in.1, s32[1,1024]{1,0:T(1,128)} %gmap_in.1), custom_call_target="tpu_custom_call" | custom-call | flops 4294967296 | bytes 8388608 | tf_op jit(solution)/shard_map/pallas_call | solution.py:315
  29.8 1.3 %copy.6 = f32[1,3,1024]{2,0,1:T(1,128)} copy(f32[1,3,1024]{2,1,0:T(4,128)} %shard_map.55) | data formatting | bytes 24576 | tf_op jit(solution)/shard_map/pallas_call | solution.py:315

commit v2 on v1

--- a/solution.py
+++ b/solution.py
@@ -58,11 +58,14 @@
     me_z, me_y = me_k // 2, me_k % 2
     other = me_z * 2 + 1 - me_y
 
+    depth_bits = depth.bit_length() - 1
+    far_first = sorted(range(1, depth), key=lambda step: step < 2)
+
     def along(step):
-        return ((me_z + step) % depth) * 2 + me_y
+        return moved(me_z, step, depth_bits) * 2 + me_y
 
     def beside(step):
-        return ((me_z + step) % depth) * 2 + 1 - me_y
+        return moved(me_z, step, depth_bits) * 2 + 1 - me_y
 
     barrier = pltpu.get_barrier_semaphore()
     peers = [(along(step), me_g) for step in range(1, depth)] + [(other, me_g)]
@@ -132,14 +135,14 @@
             device_id=(me_k, flipped(me_g, bit)), device_id_type=MESH,
         )
 
-    for step in range(1, depth):
+    for step in far_first:
         c_copy(me_k, step - 1, along(step)).start()
     c_copy(me_k, depth - 1, other).start()
     across(me_k)
     for step in range(1, depth):
         c_copy(along(step), 0, other).wait_recv()
         c_copy(along(step), depth - 1 + step, other).start()
-    for step in range(1, depth):
+    for step in far_first:
         v_copy(me_k, step - 1, along(step)).start()
     v_copy(me_k, depth - 1, other).start()
     for step in range(depth):
@@ -155,7 +158,7 @@
         pc[pl.ds(pl.multiple_of(k * rows, rows), rows), :] = dens
         return carry
 
-    lax.fori_loop(0, n_k, build, 0)
+    lax.fori_loop(0, n_k, build, 0, unroll=4)
     tiles[...] = jnp.zeros_like(tiles)
 
     sub = min(512, width)

time: 31.4 us -> 30.8 us (0.981)
  Pallas kernels: 29.8 us -> 29.2 us
    pallas_call x1, Pallas kernels: 29.8 us -> 29.2 us  [per_device(): pl.pallas_call(functools.partial(kernel, n_k, n_g), out_shape=jax.ShapeDt...]
where the time goes in v2:
time: 30.8 us; the launch traced here: 30.6 us
  Pallas kernels  29.2 us (95%)
  local copies, waits for them, and re-layouts  1.33 us (4%)
    pallas_call x1, Pallas kernels, per_device(): pl.pallas_call(functools.partial(kernel, n_k, n_g), out_shape=jax.ShapeDt...  29.2 us
    pallas_call x1, local copies, waits for them, and re-layouts, per_device(): pl.pallas_call(functools.partial(kernel, n_k, n_g), out_shape=jax.ShapeDt...  1.33 us

profile of v2, /device:TPU:0, one launch (start us, length us, event | category | flops | bytes accessed | tf_op | source)
XLA Modules:
  0.0 30.6 jit_solution(6699465044566698899)
XLA Ops:
  0.0 29.2 %shard_map.55 = f32[1,3,1024]{2,1,0:T(4,128)} custom-call(bf16[1,8,1024]{2,1,0:T(8,128)(2,1)} %cond_in.1, bf16[1,8,1024]{2,1,0:T(8,128)(2,1)} %vale_in.1, bf16[1,1024,4096]{2,1,0:T(8,128)(2,1)} %screen.1, s32[8,8]{1,0:T(8,128)} %qtable_in.1, s32[1,1024]{1,0:T(1,128)} %gmap_in.1), custom_call_target="tpu_custom_call" | custom-call | flops 4294967296 | bytes 8388608 | tf_op jit(solution)/shard_map/pallas_call | solution.py:318
  29.2 1.3 %copy.6 = f32[1,3,1024]{2,0,1:T(1,128)} copy(f32[1,3,1024]{2,1,0:T(4,128)} %shard_map.55) | data formatting | bytes 24576 | tf_op jit(solution)/shard_map/pallas_call | solution.py:318

commit v3 on v2

--- a/solution.py
+++ b/solution.py
@@ -144,9 +144,9 @@
         c_copy(along(step), depth - 1 + step, other).start()
     for step in far_first:
         v_copy(me_k, step - 1, along(step)).start()
-    v_copy(me_k, depth - 1, other).start()
     for step in range(depth):
         c_copy(beside(step), 0, other).wait_recv()
+    v_copy(me_k, depth - 1, other).start()
 
     shift = jnp.int32(0)
     for row in range(n_k):
@@ -274,7 +274,7 @@
 
             return carry
 
-        lax.fori_loop(0, group * n_g, hand_out, 0)
+        lax.fori_loop(0, group * n_g, hand_out, 0, unroll=4)
         return carry
 
     lax.fori_loop(1, n_groups + 1, finish, 0)

time: 30.8 us -> 31.3 us (1.016)
  Pallas kernels: 29.2 us -> 29.6 us
    pallas_call x1, Pallas kernels: 29.2 us -> 29.6 us  [per_device(): pl.pallas_call(functools.partial(kernel, n_k, n_g), out_shape=jax.ShapeDt...]
where the time goes in v3:
time: 31.3 us; the launch traced here: 31 us
  Pallas kernels  29.6 us (95%)
  local copies, waits for them, and re-layouts  1.33 us (4%)
    pallas_call x1, Pallas kernels, per_device(): pl.pallas_call(functools.partial(kernel, n_k, n_g), out_shape=jax.ShapeDt...  29.6 us
    pallas_call x1, local copies, waits for them, and re-layouts, per_device(): pl.pallas_call(functools.partial(kernel, n_k, n_g), out_shape=jax.ShapeDt...  1.33 us

profile of v3, /device:TPU:0, one launch (start us, length us, event | category | flops | bytes accessed | tf_op | source)
XLA Modules:
  0.0 31.0 jit_solution(7238200442454784978)
XLA Ops:
  0.0 29.6 %shard_map.55 = f32[1,3,1024]{2,1,0:T(4,128)} custom-call(bf16[1,8,1024]{2,1,0:T(8,128)(2,1)} %cond_in.1, bf16[1,8,1024]{2,1,0:T(8,128)(2,1)} %vale_in.1, bf16[1,1024,4096]{2,1,0:T(8,128)(2,1)} %screen.1, s32[8,8]{1,0:T(8,128)} %qtable_in.1, s32[1,1024]{1,0:T(1,128)} %gmap_in.1), custom_call_target="tpu_custom_call" | custom-call | flops 4294967296 | bytes 8388608 | tf_op jit(solution)/shard_map/pallas_call | solution.py:318
  29.7 1.3 %copy.6 = f32[1,3,1024]{2,0,1:T(1,128)} copy(f32[1,3,1024]{2,1,0:T(4,128)} %shard_map.55) | data formatting | bytes 24576 | tf_op jit(solution)/shard_map/pallas_call | solution.py:318

commit v4 on v2

--- a/solution.py
+++ b/solution.py
@@ -139,12 +139,12 @@
         c_copy(me_k, step - 1, along(step)).start()
     c_copy(me_k, depth - 1, other).start()
     across(me_k)
+    v_copy(me_k, depth - 1, other).start()
     for step in range(1, depth):
         c_copy(along(step), 0, other).wait_recv()
         c_copy(along(step), depth - 1 + step, other).start()
     for step in far_first:
         v_copy(me_k, step - 1, along(step)).start()
-    v_copy(me_k, depth - 1, other).start()
     for step in range(depth):
         c_copy(beside(step), 0, other).wait_recv()
 

time: 30.8 us -> 30.8 us (level)
  no operation moved by 1% of the time
where the time goes in v4:
time: 30.8 us; the launch traced here: 30.6 us
  Pallas kernels  29.2 us (95%)
  local copies, waits for them, and re-layouts  1.33 us (4%)
    pallas_call x1, Pallas kernels, per_device(): pl.pallas_call(functools.partial(kernel, n_k, n_g), out_shape=jax.ShapeDt...  29.2 us
    pallas_call x1, local copies, waits for them, and re-layouts, per_device(): pl.pallas_call(functools.partial(kernel, n_k, n_g), out_shape=jax.ShapeDt...  1.33 us

profile of v4, /device:TPU:0, one launch (start us, length us, event | category | flops | bytes accessed | tf_op | source)
XLA Modules:
  0.0 30.6 jit_solution(7704996393074810915)
XLA Ops:
  0.0 29.2 %shard_map.55 = f32[1,3,1024]{2,1,0:T(4,128)} custom-call(bf16[1,8,1024]{2,1,0:T(8,128)(2,1)} %cond_in.1, bf16[1,8,1024]{2,1,0:T(8,128)(2,1)} %vale_in.1, bf16[1,1024,4096]{2,1,0:T(8,128)(2,1)} %screen.1, s32[8,8]{1,0:T(8,128)} %qtable_in.1, s32[1,1024]{1,0:T(1,128)} %gmap_in.1), custom_call_target="tpu_custom_call" | custom-call | flops 4294967296 | bytes 8388608 | tf_op jit(solution)/shard_map/pallas_call | solution.py:318
  29.2 1.3 %copy.6 = f32[1,3,1024]{2,0,1:T(1,128)} copy(f32[1,3,1024]{2,1,0:T(4,128)} %shard_map.55) | data formatting | bytes 24576 | tf_op jit(solution)/shard_map/pallas_call | solution.py:318
